TPU v7x, 128 devices: a whole 4x4x4 slice. The times are simulated.
128 devices in a mesh: row: 8 (over x, core), col: 16 (over z, y).
Axes of the slice: x: 4, y: 4, z: 4, core: 2. Of those that a mesh axis runs over, the one named last changes fastest.
Arguments:
- flat_grad: bfloat16 [12288, 26624], P(('row', 'col')), may hold values from -6 to 6
- flat_rows: int32 [12288], P(('row', 'col')), may hold values from 0 to 12287, as said below
- momentum: bfloat16 [12288, 26624], P('row', 'col'), may hold values from -6 to 6
- basis: float32 [26624, 128], P('col'), may hold values from -0.0390625 to 0.0390625
Outputs:
- new_momentum: bfloat16 [12288, 26624], P('row', 'col')
- new_basis: float32 [26624, 128], P('col')
- flat_update: bfloat16 [12288, 26624], P(('row', 'col'))
Inputs may be any that keep to these rules, and one draw needn't show every extreme that they name: Within each aligned block of 12288 / 8 flat rows, flat_rows is a permutation of the matrix rows of that same block.
All inputs are finite; a program needn't handle non-finite values.
Results may differ from a plain program's by a relative error of at most 0.028.
Values may be sent and summed in bfloat16 or wider, within the bound.
A program may use at most 128 MiB of HBM per device.

v0:
```python
import functools
import math

import jax
import jax.numpy as jnp
from jax import lax
from jax.experimental import pallas as pl
from jax.experimental.pallas import tpu as pltpu
from jax.sharding import PartitionSpec as P

ITERS = 4
CORES = 2
STEP = 32
ROUND = 32
CHUNKS = 3
MESH = pl.DeviceIdType.MESH
BF16 = jnp.bfloat16
F32 = jnp.float32
NN = (((1,), (0,)), ((), ()))
NT = (((1,), (1,)), ((), ()))
TN = (((0,), (0,)), ((), ()))


def mm(a, b, dims=NN):
    return lax.dot_general(a, b, dims, preferred_element_type=F32)


def split(a):
    high = a.astype(BF16)
    return high, (a - high.astype(F32)).astype(BF16)


def main_kernel(
    nz, ny, nx, factor,
    grad, slots_in, mom, basis,
    merged_out, ortho_out, right_out, basis_out, o2_out, wall,
    momv, recv, merged, turned, perm, perm_t, named_in, slots, current, rs_send, rs_recv, left, gram_own, gram_pair, gram_x, gram_all, w_send, w_pair, w_mid, w_recv, wag,
    w_sum, squares, rightf, ortho, amat, xmat, linv, mom_sem, out_sem, slot_s, slot_r, grad_s, grad_r,
    rs_s, rs_r, sq_s, sq_r, ag_s, ag_r, gram_s, gram_r, wrs_s, wrs_r, xrs_s, xrs_r, wag_s, wag_r, wall_s, wall_r, pair_s, pair_r,
    half_s, half_r, own_sem, last_s, last_r,
):
    row, col = lax.axis_index("row"), lax.axis_index("col")
    z, y = col // ny, col % ny
    x, core = row // CORES, row % CORES
    n_col, n_row = nz * ny, nx * CORES
    tile_rows, tile_cols = merged.shape
    rank = current.shape[1]
    flat = tile_rows // n_col
    rounds, per_round = flat // ROUND, n_col * ROUND
    group = flat * ny
    piece = tile_cols // n_row
    quarter = tile_cols // 4
    half = tile_cols // CORES
    offsets = [(dz, dy) for dz in range(nz) for dy in range(ny) if (dz, dy) != (0, 0)]
    offsets.sort(key=lambda o: (min(o[0], nz - o[0]) + min(o[1], ny - o[1]), max(o)))
    far_first = offsets[::-1]
    across = sorted(range(1, nx), key=lambda d: -min(d, nx - d))
    partner = x * CORES + (1 - core)

    def shifted(dz, dy):
        return lax.rem(z + dz, nz) * ny + lax.rem(y + dy, ny)

    def beside(dx):
        return lax.rem(x + dx, nx) * CORES + core

    def rows_at(index, size):
        return pl.ds(pl.multiple_of(index * size, size), size)

    def remote(src, dst, send, receive, to_row, to_col):
        return pltpu.make_async_remote_copy(
            src_ref=src, dst_ref=dst, send_sem=send, recv_sem=receive, device_id=(to_row, to_col), device_id_type=MESH
        )

    def await_recv(ref, sem):
        remote(ref, ref, sem, sem, partner, col).wait_recv()

    def await_send(ref, sem):
        remote(ref, ref, sem, sem, partner, col).wait_send()

    load = pltpu.make_async_copy(mom, momv, mom_sem)
    load.start()
    load_basis = pltpu.make_async_copy(basis, rightf, half_s.at[0])
    load_basis.start()
    load_slots = pltpu.make_async_copy(slots_in, named_in, half_s.at[1])
    load_slots.start()
    squares[...] = jnp.zeros_like(squares)

    barrier = pltpu.get_barrier_semaphore()
    for dz, dy in offsets:
        pl.semaphore_signal(barrier, inc=1, device_id=(row, shifted(dz, dy)), device_id_type=MESH)
    for dx in range(1, nx):
        pl.semaphore_signal(barrier, inc=1, device_id=(beside(dx), col), device_id_type=MESH)
    pl.semaphore_signal(barrier, inc=1, device_id=(partner, col), device_id_type=MESH)
    pl.semaphore_wait(barrier, n_col - 1 + nx)

    slots[col] = jnp.zeros((8, 128), jnp.int32)
    load_slots.wait()
    slots[col, 0:1, 0:flat] = named_in[...]
    for dz, dy in offsets:
        remote(slots.at[col], slots.at[col], slot_s, slot_r, row, shifted(dz, dy)).start()

    def columns_of(c):
        return pl.ds(pl.multiple_of(c * tile_cols, 128), tile_cols)

    def row_of(r, c):
        return pl.ds(pl.multiple_of(r * per_round + c * ROUND, ROUND), ROUND)

    own = []
    for r in range(rounds):
        taken = pl.ds(r * ROUND, ROUND)
        for dz, dy in offsets:
            to = shifted(dz, dy)
            remote(
                grad.at[taken, columns_of(to)], recv.at[row_of(r, col), :], grad_s, grad_r.at[r], row, to
            ).start()
        own.append(
            pltpu.make_async_copy(grad.at[taken, columns_of(col)], recv.at[row_of(r, col), :], own_sem.at[r])
        )
        own[r].start()

    load_basis.wait()
    current[...] = rightf[...].astype(BF16)
    await_recv(slots.at[pl.ds(0, n_col - 1)], slot_r)
    await_send(slots.at[pl.ds(0, n_col - 1)], slot_s)

    def fill_perm(c, _):
        named = jnp.broadcast_to(slots[c][0:1, :], (128, 128)).T - row * tile_rows
        lanes = lax.broadcasted_iota(jnp.int32, (ROUND, 128), 1)
        for r in range(rounds):
            part = named[r * ROUND : (r + 1) * ROUND]
            for t in range(tile_rows // 128):
                perm[row_of(r, c), t * 128 : (t + 1) * 128] = jnp.where(part == lanes + t * 128, 1.0, 0.0).astype(BF16)
        return 0

    lax.fori_loop(0, n_col, fill_perm, 0)
    load.wait()

    wide = 256
    n_wide, rest = tile_cols // wide, tile_cols % wide

    def permute(target, one, source, at):
        block = one[at, :]

        def part(t, _):
            cols = rows_at(t, wide)
            target[at, cols] = mm(block, source[:, cols]).astype(BF16)
            return 0

        lax.fori_loop(0, n_wide, part, 0)
        if rest:
            cols = pl.ds(n_wide * wide, rest)
            target[at, cols] = mm(block, source[:, cols]).astype(BF16)

    def permute_group(g, _):
        permute(merged, perm, momv, rows_at(g, group))
        return 0

    lax.fori_loop(0, nz, permute_group, 0)

    def turn_perm(t, _):
        cols = rows_at(t, 128)
        perm_t[cols, :] = perm[:, cols].T
        return 0

    lax.fori_loop(0, tile_rows // 128, turn_perm, 0)

    for r in range(rounds):
        begin = r * per_round
        own[r].wait()
        await_recv(recv.at[pl.ds(0, (n_col - 1) * ROUND), :], grad_r.at[r])

        def add(i, _, begin=begin):
            at = pl.ds(pl.multiple_of(begin + i * ROUND, ROUND), ROUND)
            merged[at, :] = (merged[at, :].astype(F32) + recv[at, :].astype(F32)).astype(BF16)
            return 0

        lax.fori_loop(0, n_col, add, 0)

        def turn(t, _, begin=begin):
            cols = rows_at(t, 128)
            turned[cols, begin : begin + per_round] = merged[begin : begin + per_round, cols].T
            return 0

        lax.fori_loop(0, tile_cols // 128, turn, 0)
    await_send(recv.at[pl.ds(0, (n_col - 1) * flat), :], grad_s)

    lane = lax.broadcasted_iota(jnp.int32, (STEP, rank), 1)
    sub = lax.broadcasted_iota(jnp.int32, (STEP, rank), 0)

    def eliminate(b, _):
        start = b * STEP
        at = rows_at(b, STEP)
        a, v = amat[at, :], xmat[at, :]
        spread = [
            jnp.broadcast_to(jnp.sum(jnp.where(lane == start + k, a, 0.0), axis=1, keepdims=True), (STEP, rank))
            for k in range(STEP)
        ]
        inverse = jnp.ones((STEP, rank), F32)
        for k in range(STEP):
            one_over = 1.0 / jnp.broadcast_to(spread[k][k : k + 1, :], (STEP, rank))
            inverse = jnp.where(sub == k, one_over, inverse)
            if k < STEP - 1:
                ratio = jnp.where(sub > k, spread[k] * one_over, 0.0)
                a = a - ratio * jnp.broadcast_to(a[k : k + 1, :], (STEP, rank))
                v = v - ratio * jnp.broadcast_to(v[k : k + 1, :], (STEP, rank))
                for j in range(k + 1, STEP):
                    spread[j] = spread[j] - ratio * jnp.broadcast_to(spread[j][k : k + 1, :], (STEP, rank))
        linv[at, :] = v * jnp.sqrt(inverse)
        scaled = jnp.where(lane >= start + STEP, a * inverse, 0.0)
        change = lax.dot_general(
            scaled,
            jnp.concatenate([a, v], axis=1),
            TN,
            precision=lax.Precision.HIGHEST,
            preferred_element_type=F32,
        )
        amat[...] -= change[:, :rank]
        xmat[...] -= change[:, rank:]
        return 0

    steps = rank // STEP
    chunk, share = tile_rows // CHUNKS, flat // CHUNKS
    restored = tile_rows // (2 * ITERS)

    def share_of(h, c):
        return pl.ds(pl.multiple_of(h * chunk + c * share, share), share)

    def others(ref, h):
        return ref.at[pl.ds(h * (n_col - 1) * share, (n_col - 1) * share), :]

    gram_half = rank // CORES

    sizes = [(piece // 2 + 15) // 16 * 16]
    sizes.append(piece - sizes[0])
    PARTS = (0, 1)

    def half_rows(e, c):
        return pl.ds(pl.multiple_of(e * n_row * sizes[0] + c * nx * sizes[e], 16), nx * sizes[e])

    def held(e, xc):
        return pl.ds(pl.multiple_of(e * n_row * sizes[0] + (core * nx + xc) * sizes[e], 16), sizes[e])

    def mid_rows(e, xc):
        return pl.ds(pl.multiple_of(e * nx * sizes[0] + xc * sizes[e], 16), sizes[e])

    def mid_part(e):
        return pl.ds(e * nx * sizes[0], nx * sizes[e])

    def recv_rows(e, i):
        return pl.ds(e * (nx - 1) * sizes[0] + i * sizes[e], sizes[e])

    def recv_part(e):
        return pl.ds(e * (nx - 1) * sizes[0], (nx - 1) * sizes[e])


    def iterate(k, _):
        for h in range(CHUNKS):
            at = slice(h * chunk, (h + 1) * chunk)
            rs_send[at, :] = mm(merged[at, :], current[...]).astype(BF16)
            for i, (dz, dy) in enumerate(far_first):
                to = shifted(dz, dy)
                slot = pl.ds((h * (n_col - 1) + i) * share, share)
                remote(rs_send.at[share_of(h, to), :], rs_recv.at[slot, :], rs_s.at[h], rs_r.at[h], row, to).start()
            if h == 0:
                for dz, dy in offsets:
                    to = shifted(dz, dy)
                    remote(squares.at[col, pl.ds(0, 1)], squares.at[col, pl.ds(0, 1)], sq_s, sq_r, row, to).start()
        permute(momv, perm_t, merged, rows_at(2 * k, restored))
        await_recv(squares.at[pl.ds(0, n_col - 1), pl.ds(0, 1)], sq_r)
        norm = jnp.sqrt(jnp.sum(squares[:, 0:1, :], axis=0) + 1e-06)
        scale = 1.0 / jnp.where(k == 0, jnp.ones_like(norm), norm)
        for h in range(CHUNKS):
            await_recv(others(rs_recv, h), rs_r.at[h])
            total = rs_send[share_of(h, col), :].astype(F32)
            for i in range(n_col - 1):
                begin = (h * (n_col - 1) + i) * share
                total = total + rs_recv[begin : begin + share, :].astype(F32)
            left[share_of(h, col), :] = (total * scale).astype(BF16)
            for dz, dy in far_first:
                ours = left.at[share_of(h, col), :]
                remote(ours, ours, ag_s.at[h], ag_r.at[h], row, shifted(dz, dy)).start()
        xmat[...] = jnp.where(
            lax.broadcasted_iota(jnp.int32, (rank, rank), 0) == lax.broadcasted_iota(jnp.int32, (rank, rank), 1), 1.0, 0.0
        )
        await_send(squares.at[pl.ds(0, n_col - 1), pl.ds(0, 1)], sq_s)
        for h in range(CHUNKS):
            await_send(others(rs_recv, h), rs_s.at[h])

        for h in range(CHUNKS):
            at = slice(h * chunk, (h + 1) * chunk)
            await_recv(others(rs_recv, h), ag_r.at[h])
            gram_part = mm(left[at, :], left[at, :], TN)
            gram_own[...] = gram_part if h == 0 else gram_own[...] + gram_part
            if h < CHUNKS - 1:
                w_part = mm(turned[:, at], left[at, :])
                w_sum[...] = w_part if h == 0 else w_sum[...] + w_part
        final = slice((CHUNKS - 1) * chunk, CHUNKS * chunk)
        to_pair = remote(gram_own, gram_pair, gram_s, gram_r, partner, col)
        to_pair.start()
        w_to_pair = []
        for e in PARTS:
            at = half_rows(e, 1 - core)
            here = mid_part(e)
            w_send[here, :] = (w_sum[at, :] + mm(turned[at, final], left[final, :])).astype(BF16)
            w_to_pair.append(
                remote(w_send.at[here, :], w_pair.at[here, :], wrs_s.at[e], wrs_r.at[e], partner, col)
            )
            w_to_pair[e].start()
        await_recv(gram_pair, gram_r)
        gram_rows = rows_at(core, gram_half)
        gram_x[x] = gram_own[gram_rows, :] + gram_pair[gram_rows, :]
        for dx in across:
            remote(gram_x.at[x], gram_x.at[x], half_s.at[0], half_r.at[0], beside(dx), col).start()
        for e in PARTS:
            at = half_rows(e, core)
            here = mid_part(e)
            own_half = w_sum[at, :] + mm(turned[at, final], left[final, :])
            await_recv(w_pair.at[here, :], wrs_r.at[e])
            w_mid[here, :] = (own_half + w_pair[here, :].astype(F32)).astype(BF16)
            for dx in across:
                to = lax.rem(x + dx, nx)
                slot = w_recv.at[recv_rows(e, dx - 1), :]
                remote(w_mid.at[mid_rows(e, to), :], slot, xrs_s.at[e], xrs_r.at[e], beside(dx), col).start()
        for h in range(CHUNKS):
            await_send(others(rs_recv, h), ag_s.at[h])
        permute(momv, perm_t, merged, rows_at(2 * k + 1, restored))
        await_recv(gram_x.at[pl.ds(0, nx - 1)], half_r.at[0])
        gram = gram_x[0]
        for d in range(1, nx):
            gram = gram + gram_x[d]
        gram_all[gram_rows, :] = gram
        halves = remote(gram_all.at[gram_rows, :], gram_all.at[gram_rows, :], half_s.at[1], half_r.at[1], partner, col)
        halves.start()
        for e in PARTS:
            await_recv(w_recv.at[recv_part(e), :], xrs_r.at[e])
            total = w_mid[mid_rows(e, x), :].astype(F32)
            for d in range(nx - 1):
                total = total + w_recv[recv_rows(e, d), :].astype(F32)
            wag[held(e, x), :] = total.astype(BF16)
            ours = wag.at[held(e, x), :]
            for dx in across:
                remote(ours, ours, wag_s, wag_r.at[e, x], beside(dx), col).start()
            remote(ours, ours, pair_s, pair_r.at[e], partner, col).start()
            if e == 0:
                await_recv(gram_all.at[gram_rows, :], half_r.at[1])
                amat[...] = gram_all[...]
        lax.fori_loop(0, 2, eliminate, 0)
        for e in PARTS:
            for dx in range(1, nx):
                xc = lax.rem(x + dx, nx)
                theirs = wag.at[held(e, xc), :]
                await_recv(theirs, wag_r.at[e, xc])
                remote(theirs, theirs, pair_s, pair_r.at[e], partner, col).start()
            if e == 0:
                lax.fori_loop(2, steps - 1, eliminate, 0)
        lax.fori_loop(steps - 1, steps, eliminate, 0)

        high, low = split(linv[...])

        def right_of(at):
            part = mm(wag[at, :], high, NT) + mm(wag[at, :], low, NT)
            rightf[at, :] = part
            current[at, :] = part.astype(BF16)
            return jnp.sum(part * part, axis=0, keepdims=True)

        near_sum = right_of(half_rows(0, core)) + right_of(half_rows(1, core))
        to_pair.wait_send()
        for e in PARTS:
            w_to_pair[e].wait_send()
            await_send(w_recv.at[recv_part(e), :], xrs_s.at[e])
        await_send(gram_x.at[pl.ds(0, nx - 1)], half_s.at[0])
        halves.wait_send()
        await_send(w_recv, wag_s)
        far_sum = []
        for e in PARTS:
            await_recv(w_pair.at[mid_part(e), :], pair_r.at[e])
            far_sum.append(right_of(half_rows(e, 1 - core)))
        summed = near_sum + (far_sum[0] + far_sum[1])
        await_send(w_pair, pair_s)
        squares[col] = jnp.broadcast_to(summed, (8, rank))
        return 0

    lax.fori_loop(0, ITERS, iterate, 0)

    store = pltpu.make_async_copy(momv, merged_out, mom_sem)
    store.start()

    def turn_right(t, _):
        at = rows_at(t, 128)
        right_out[:, at] = current[at, :].T
        return 0

    lax.fori_loop(0, tile_cols // 128, turn_right, 0)

    rank_part = rank // 4

    def cut(c, p):
        return pl.ds(pl.multiple_of((core * 2 + p) * rank_part, rank_part), rank_part), columns_of(c)

    def cut_half(c, p, h):
        size = rank_part // 2
        return pl.ds(pl.multiple_of((core * 2 + p) * rank_part + h * size, size), size), columns_of(c)

    def along(p, a, b):
        return shifted(a, b) if p == 0 else shifted(b, a)

    def send_own(p, to):
        part, cols = cut(col, p)
        remote(right_out.at[part, :], wall.at[part, cols], wall_s, wall_r.at[p, col], row, to).start()

    def send_part(at, p, c, to):
        remote(wall.at[at], wall.at[at], wall_s, wall_r.at[p, c], row, to).start()

    def to_partner(p, c):
        remote(wall.at[cut(c, p)], wall.at[cut(c, p)], last_s, last_r, partner, col).start()

    near = (1, ny - 1) if ny == 4 else tuple(range(1, ny))
    far = (2,) if ny == 4 else ()

    def pass_near(p, c, axis, d):
        if far:
            to = along(p, ny - d, 0) if axis == 0 else along(p, 0, ny - d)
            send_part(cut_half(c, p, 0 if d == 1 else 1), p, c, to)

    def spread_second(p, c):
        for d in near:
            send_part(cut(c, p), p, c, along(p, 0, d))

    def arrived(p, a, b):
        c = along(p, a, b)
        await_recv(wall.at[cut(c, p)], wall_r.at[p, c])
        return c

    write = pltpu.make_async_copy(right_out, wall.at[:, columns_of(col)], out_sem)
    write.start()
    for p in range(2):
        for d in near:
            send_own(p, along(p, d, 0))
    for p in range(2):
        for d in near:
            send_own(p, along(p, 0, d))
    for dz, dy in offsets:
        remote(squares.at[col, pl.ds(0, 1)], squares.at[col, pl.ds(0, 1)], sq_s, sq_r, row, shifted(dz, dy)).start()
    high, low = split(linv[...])
    ortho[...] = (mm(left[...], high, NT) + mm(left[...], low, NT)).astype(BF16)
    for a in near:
        for p in range(2):
            c = arrived(p, a, 0)
            pass_near(p, c, 0, a)
            spread_second(p, c)
            to_partner(p, c)
    for b in near:
        for p in range(2):
            c = arrived(p, 0, b)
            pass_near(p, c, 1, b)
            to_partner(p, c)
    for a in far:
        for p in range(2):
            c = arrived(p, a, 0)
            spread_second(p, c)
            to_partner(p, c)
    await_recv(squares.at[pl.ds(0, n_col - 1), pl.ds(0, 1)], sq_r)
    await_send(squares.at[pl.ds(0, n_col - 1), pl.ds(0, 1)], sq_s)
    norm = jnp.sqrt(jnp.sum(squares[:, 0:1, :], axis=0) + 1e-06)
    basis_out[...] = rightf[...] / norm
    for r in range(rounds):
        o2_out[r * ROUND : (r + 1) * ROUND, :] = (ortho[row_of(r, col), :].astype(F32) * (factor / norm)).astype(BF16)
    for a in near:
        for b in near:
            for p in range(2):
                c = arrived(p, a, b)
                pass_near(p, c, 1, b)
                to_partner(p, c)
    ortho_out[...] = mm(perm_t[...], ortho[...]).astype(BF16)
    for b in far:
        for p in range(2):
            to_partner(p, arrived(p, 0, b))
    for a in far:
        for b in near:
            for p in range(2):
                c = arrived(p, a, b)
                pass_near(p, c, 1, b)
                to_partner(p, c)
    for a in near + far:
        for b in far:
            for p in range(2):
                to_partner(p, arrived(p, a, b))
    most = pl.ds(0, 2 * rank_part), pl.ds(0, (n_col - 1) * tile_cols)
    await_recv(wall.at[most], last_r)
    await_send(wall.at[most], last_s)
    await_send(wall.at[most], wall_s)
    store.wait()
    write.wait()


def output_kernel(
    parts, o2, ortho, right, merged, basis, wall, new_momentum, update, new_basis, wall_v, sum_v, update_v, in_sem, out_sem
):
    flat, cols = update.shape
    tile_rows = merged.shape[0]
    some_rows, some_cols = tile_rows // parts, cols // parts
    loads, stores = [], [pltpu.make_async_copy(basis, new_basis, out_sem.at[2, 0])]
    for i in range(parts):
        at, of = pl.ds(i * some_rows, some_rows), pl.ds(i * some_cols, some_cols)
        loads.append(pltpu.make_async_copy(wall.at[:, of], wall_v.at[:, of], in_sem.at[i]))
        stores.append(pltpu.make_async_copy(sum_v.at[at, :], new_momentum.at[at, :], out_sem.at[0, i]))
        stores.append(pltpu.make_async_copy(update_v.at[:, of], update.at[:, of], out_sem.at[1, i]))
    for load in loads:
        load.start()
    stores[0].start()
    for i in range(parts):
        at, of = pl.ds(i * some_rows, some_rows), pl.ds(i * some_cols, some_cols)
        fed_back = mm(ortho[at, :], right[...])
        sum_v[at, :] = (merged[at, :].astype(F32) - 0.05 * fed_back).astype(BF16)
        stores[2 * i + 1].start()
        loads[i].wait()
        update_v[:, of] = mm(o2[...], wall_v[:, of]).astype(BF16)
        stores[2 * i + 2].start()
    for store in stores:
        store.wait()


def shards(nz, ny, nx, flat_grad, flat_rows, momentum, basis):
    tile_rows, tile_cols = momentum.shape
    flat, cols = flat_grad.shape
    rank = basis.shape[1]
    n_col, n_row = nz * ny, nx * CORES
    piece = tile_cols // n_row
    half = tile_cols // CORES
    factor = math.sqrt(tile_rows * n_row * cols / rank)
    dma = pltpu.SemaphoreType.DMA
    any_space = pl.BlockSpec(memory_space=pl.ANY)
    vmem = pl.BlockSpec(memory_space=pltpu.VMEM)
    hbm = pl.BlockSpec(memory_space=pltpu.HBM)
    shape = jax.ShapeDtypeStruct
    merged, ortho, right, new_basis, o2, wall = pl.pallas_call(
        functools.partial(main_kernel, nz, ny, nx, factor),
        out_shape=[
            shape((tile_rows, tile_cols), BF16),
            shape((tile_rows, rank), BF16),
            shape((rank, tile_cols), BF16),
            shape((tile_cols, rank), F32),
            shape((flat, rank), BF16),
            shape((rank, cols), BF16),
        ],
        in_specs=[hbm, hbm, hbm, hbm],
        out_specs=[any_space, vmem, vmem, vmem, vmem, any_space],
        scratch_shapes=[
            pltpu.VMEM((tile_rows, tile_cols), BF16),
            pltpu.VMEM((tile_rows, tile_cols), BF16),
            pltpu.VMEM((tile_rows, tile_cols), BF16),
            pltpu.VMEM((tile_cols, tile_rows), BF16),
            pltpu.VMEM((tile_rows, tile_rows), BF16),
            pltpu.VMEM((tile_rows, tile_rows), BF16),
            pltpu.VMEM((1, flat), jnp.int32),
            pltpu.VMEM((n_col, 8, 128), jnp.int32),
            pltpu.VMEM((tile_cols, rank), BF16),
            pltpu.VMEM((tile_rows, rank), BF16),
            pltpu.VMEM(((n_col - 1) * flat, rank), BF16),
            pltpu.VMEM((tile_rows, rank), BF16),
            pltpu.VMEM((rank, rank), F32),
            pltpu.VMEM((rank, rank), F32),
            pltpu.VMEM((nx, rank // CORES, rank), F32),
            pltpu.VMEM((rank, rank), F32),
            pltpu.VMEM((half, rank), BF16),
            pltpu.VMEM((half, rank), BF16),
            pltpu.VMEM((half, rank), BF16),
            pltpu.VMEM(((nx - 1) * piece, rank), BF16),
            pltpu.VMEM((tile_cols, rank), BF16),
            pltpu.VMEM((tile_cols, rank), F32),
            pltpu.VMEM((n_col, 8, rank), F32),
            pltpu.VMEM((tile_cols, rank), F32),
            pltpu.VMEM((tile_rows, rank), BF16),
            pltpu.VMEM((rank, rank), F32),
            pltpu.VMEM((rank, rank), F32),
            pltpu.VMEM((rank, rank), F32),
            dma, dma,
            dma, dma,
            dma, dma((flat // ROUND,)),
            dma((CHUNKS,)), dma((CHUNKS,)), dma, dma, dma((CHUNKS,)), dma((CHUNKS,)),
            dma, dma, dma((2,)), dma((2,)), dma((2,)), dma((2,)), dma, dma((2, nx)),
            dma, dma((2, n_col)),
            dma, dma((2,)),
            dma((2,)), dma((2,)),
            dma((flat // ROUND,)),
            dma, dma,
        ],
        compiler_params=pltpu.CompilerParams(
            collective_id=0, has_side_effects=True, vmem_limit_bytes=42 * 1024 * 1024
        ),
        name="dion_main",
    )(flat_grad, flat_rows.reshape(1, flat), momentum, basis)

    parts = 8
    new_momentum, update, new_basis = pl.pallas_call(
        functools.partial(output_kernel, parts),
        out_shape=[
            shape((tile_rows, tile_cols), BF16),
            shape((flat, cols), BF16),
            shape((tile_cols, rank), F32),
        ],
        in_specs=[vmem, vmem, vmem, vmem, vmem, any_space],
        out_specs=[any_space, any_space, any_space],
        scratch_shapes=[
            pltpu.VMEM((rank, cols), BF16),
            pltpu.VMEM((tile_rows, tile_cols), BF16),
            pltpu.VMEM((flat, cols), BF16),
            dma((parts,)),
            dma((3, parts)),
        ],
        compiler_params=pltpu.CompilerParams(vmem_limit_bytes=44 * 1024 * 1024),
        name="dion_outputs",
    )(o2, ortho, right, merged, new_basis, wall)
    return new_momentum, new_basis, update


def solution(mesh):
    n_row, n_col = mesh.shape["row"], mesh.shape["col"]
    ny = math.isqrt(n_col)
    return jax.shard_map(
        functools.partial(shards, n_col // ny, ny, n_row // CORES),
        mesh=mesh,
        in_specs=(P(("row", "col"), None), P(("row", "col")), P("row", "col"), P("col", None)),
        out_specs=(P("row", "col"), P("col", None), P(("row", "col"), None)),
        check_vma=False,
    )
```

profile of v0, /device:TPU:1, one launch (start us, length us, event | category | flops | bytes accessed | tf_op | source)
XLA Modules:
  0.0 216.3 jit_solution(8225387968311681942)
XLA Ops:
  0.6 0.0 copy-start
  0.6 1.1 copy-done
  1.8 0.0 copy-start.1
  1.8 0.7 copy-done.1
  2.4 207.0 %dion_main.1 = (bf16[1536,1664]{1,0:T(8,128)(2,1)S(1)}, bf16[1536,128]{1,0:T(8,128)(2,1)S(1)}, bf16[128,1664]{1,0:T(8,128)(2,1)S(1)}, f32[1664,128]{1,0:T(8,128)...) custom-call(bf16[96,26624]{1,0:T(8,128)(2,1)} %grad.1, s32[1,96]{1,0:T(1,128)S(1)} %bitcast.1, ...), custom_call_target="tpu_custom_call" | custom-call | tf_op jit(solution)/shard_map/dion_main/pallas_call | solution.py:536
  209.4 6.7 %dion_outputs.1 = (bf16[1536,1664]{1,0:T(8,128)(2,1)}, bf16[96,26624]{1,0:T(8,128)(2,1)}, f32[1664,128]{1,0:T(8,128)}) custom-call(bf16[96,128]{1,0:T(8,128)(2,1)S(1)} %get-tuple-element.12.o2, bf16[1536,128]{1,0:T(8,128)(2,1)S(1)} %get-tuple-element.13.ortho, bf16[128,1664]{1,0:T(8,128)(2,1)S(1)} %get-tuple-element.14.right, ...), custom_call_target="tpu_custom_call" | custom-call | tf_op jit(solution)/shard_map/dion_outputs/pallas_call | solution.py:595
Async XLA Ops:
  0.6 1.2 copy-start
  1.8 0.7 copy-start.1
where the time goes:
time: 216 us
  Pallas kernels  214 us (99%)
    pallas_call x1, Pallas kernels, shards(): pl.pallas_call(functools.partial(main_kernel, nz, ny, nx, factor), out_sh...  207 us
    pallas_call x1, Pallas kernels, shards(): pl.pallas_call(functools.partial(output_kernel, parts), out_shape=[shape(...  6.71 us

commit v1 on v0

--- a/solution.py
+++ b/solution.py
@@ -187,7 +187,7 @@
     lane = lax.broadcasted_iota(jnp.int32, (STEP, rank), 1)
     sub = lax.broadcasted_iota(jnp.int32, (STEP, rank), 0)
 
-    def eliminate(b, _):
+    def eliminate(b, _, last=False):
         start = b * STEP
         at = rows_at(b, STEP)
         a, v = amat[at, :], xmat[at, :]
@@ -206,6 +206,8 @@
                 for j in range(k + 1, STEP):
                     spread[j] = spread[j] - ratio * jnp.broadcast_to(spread[j][k : k + 1, :], (STEP, rank))
         linv[at, :] = v * jnp.sqrt(inverse)
+        if last:
+            return 0
         scaled = jnp.where(lane >= start + STEP, a * inverse, 0.0)
         change = lax.dot_general(
             scaled,
@@ -344,7 +346,8 @@
             if e == 0:
                 await_recv(gram_all.at[gram_rows, :], half_r.at[1])
                 amat[...] = gram_all[...]
-        lax.fori_loop(0, 2, eliminate, 0)
+                lax.fori_loop(0, 1, eliminate, 0)
+        lax.fori_loop(1, 2, eliminate, 0)
         for e in PARTS:
             for dx in range(1, nx):
                 xc = lax.rem(x + dx, nx)
@@ -353,7 +356,7 @@
                 remote(theirs, theirs, pair_s, pair_r.at[e], partner, col).start()
             if e == 0:
                 lax.fori_loop(2, steps - 1, eliminate, 0)
-        lax.fori_loop(steps - 1, steps, eliminate, 0)
+        eliminate(steps - 1, 0, last=True)
 
         high, low = split(linv[...])
 

time: 216 us -> 216 us (level)
  no operation moved by 1% of the time
where the time goes in v1:
time: 216 us
  Pallas kernels  213 us (99%)
    pallas_call x1, Pallas kernels, shards(): pl.pallas_call(functools.partial(main_kernel, nz, ny, nx, factor), out_sh...  206 us
    pallas_call x1, Pallas kernels, shards(): pl.pallas_call(functools.partial(output_kernel, parts), out_shape=[shape(...  6.71 us

profile of v1, /device:TPU:1, one launch (start us, length us, event | category | flops | bytes accessed | tf_op | source)
XLA Modules:
  0.0 215.8 jit_solution(2030297992771620373)
XLA Ops:
  0.6 0.0 copy-start
  0.6 1.1 copy-done
  1.8 0.0 copy-start.1
  1.8 0.7 copy-done.1
  2.4 206.5 %dion_main.1 = (bf16[1536,1664]{1,0:T(8,128)(2,1)S(1)}, bf16[1536,128]{1,0:T(8,128)(2,1)S(1)}, bf16[128,1664]{1,0:T(8,128)(2,1)S(1)}, f32[1664,128]{1,0:T(8,128)...) custom-call(bf16[96,26624]{1,0:T(8,128)(2,1)} %grad.1, s32[1,96]{1,0:T(1,128)S(1)} %bitcast.1, ...), custom_call_target="tpu_custom_call" | custom-call | tf_op jit(solution)/shard_map/dion_main/pallas_call | solution.py:539
  209.0 6.7 %dion_outputs.1 = (bf16[1536,1664]{1,0:T(8,128)(2,1)}, bf16[96,26624]{1,0:T(8,128)(2,1)}, f32[1664,128]{1,0:T(8,128)}) custom-call(bf16[96,128]{1,0:T(8,128)(2,1)S(1)} %get-tuple-element.12.o2, bf16[1536,128]{1,0:T(8,128)(2,1)S(1)} %get-tuple-element.13.ortho, bf16[128,1664]{1,0:T(8,128)(2,1)S(1)} %get-tuple-element.14.right, ...), custom_call_target="tpu_custom_call" | custom-call | tf_op jit(solution)/shard_map/dion_outputs/pallas_call | solution.py:598
Async XLA Ops:
  0.6 1.2 copy-start
  1.8 0.7 copy-start.1
